TPU v7x, 32 devices: a whole 2x2x4 slice. The times are simulated.
32 devices in a mesh: dp: 2 (over y), gx: 8 (over z, x), gy: 2 (over core).
Axes of the slice: x: 2, y: 2, z: 4, core: 2. Of those that a mesh axis runs over, the one named last changes fastest.
Arguments:
- fields: bfloat16 [2, 16, 256, 32768], P('dp', None, 'gx', 'gy'), may hold values from -6 to 6
- pre_act: bfloat16 [2, 16, 256, 32768], P('dp', None, 'gx', 'gy'), may hold values from -6 to 6
- cotangent: bfloat16 [2, 16, 256, 32768], P('dp', None, 'gx', 'gy'), may hold values from -6 to 6
- spec_weight: bfloat16 [2, 32, 32, 16, 256], P(None, 'gx', None, 'gy'), may hold values from -12 to 12
- point_weight: bfloat16 [16, 16], replicated, may hold values from -1.5 to 1.5
Outputs:
- grad_fields: bfloat16 [2, 16, 256, 32768], P('dp', None, 'gx', 'gy')
- grad_spec: float32 [2, 32, 32, 16, 256], P(None, 'gx', None, 'gy')
All inputs are finite; a program needn't handle non-finite values.
Results may differ from a plain program's by a relative error of at most 0.0098.
Values may be sent and summed in bfloat16 or wider, within the bound.
A program may use at most 320 MiB of HBM per device.

v0:
```python
import math

import jax
import jax.numpy as jnp
from jax import lax
from jax.sharding import PartitionSpec as P

C = 16
NX = 256
NY = 512
NZ = 64
MX = 32
MY = 32
MZ = 16


def kept_freqs(kept, length, both_signs):
    index = jnp.arange(kept, dtype=jnp.int32)
    if both_signs:
        return jnp.where(index < kept // 2, index, length - kept + index)
    return index


def phase(freqs, points, length):
    turns = points[:, None] * freqs[None, :] % length
    return turns.astype(jnp.float32) * (2.0 * math.pi / length)


def forward_table(kept, length):
    angle = phase(kept_freqs(kept, length, True), jnp.arange(length, dtype=jnp.int32), length)
    cosine = jnp.cos(angle)
    minus_sine = -jnp.sin(angle)
    upper = jnp.stack([cosine, minus_sine], axis=-1)
    lower = jnp.stack([-minus_sine, cosine], axis=-1)
    return jnp.stack([upper, lower], axis=1).astype(jnp.bfloat16)


def inverse_table(kept, length, positions):
    angle = phase(kept_freqs(kept, length, True), positions, length)
    cosine = jnp.transpose(jnp.cos(angle))
    sine = jnp.transpose(jnp.sin(angle))
    upper = jnp.stack([cosine, sine], axis=-1)
    lower = jnp.stack([-sine, cosine], axis=-1)
    return jnp.stack([upper, lower], axis=1).astype(jnp.bfloat16)


def z_forward_table():
    angle = phase(kept_freqs(MZ, NZ, False), jnp.arange(NZ, dtype=jnp.int32), NZ)
    return (
        jnp.stack([jnp.cos(angle), -jnp.sin(angle)], axis=-1)
        .reshape(NZ, 2 * MZ)
        .astype(jnp.bfloat16)
    )


def z_inverse_table():
    angle = jnp.transpose(phase(kept_freqs(MZ, NZ, False), jnp.arange(NZ, dtype=jnp.int32), NZ))
    return (
        jnp.stack([jnp.cos(angle), -jnp.sin(angle)], axis=1)
        .reshape(2 * MZ, NZ)
        .astype(jnp.bfloat16)
    )


def gelu_slope(value):
    cdf = 0.5 * (1.0 + jax.scipy.special.erf(value * (1.0 / math.sqrt(2.0))))
    return cdf + value * jnp.exp(-0.5 * value * value) * (1.0 / math.sqrt(2.0 * math.pi))


def scale_modes(mode_values, weight_z):
    return mode_values.astype(jnp.float32) * weight_z[:, None]


def weight_grads(field_hat, grad_scaled):
    highest = lax.Precision.HIGHEST
    real_u = field_hat[..., 0].astype(jnp.float32)
    imag_u = field_hat[..., 1].astype(jnp.float32)
    real_d = grad_scaled[..., 0]
    imag_d = grad_scaled[..., 1]
    form = "bixyz,boxyz->xyzio"
    real_w = jnp.einsum(form, real_u, real_d, precision=highest) + jnp.einsum(
        form, imag_u, imag_d, precision=highest
    )
    imag_w = jnp.einsum(form, real_u, imag_d, precision=highest) - jnp.einsum(
        form, imag_u, real_d, precision=highest
    )
    result = jnp.stack([real_w, imag_w], axis=0)
    return result.reshape(result.shape[:4] + (C * C,))


def input_grads(spec_weight, grad_scaled):
    highest = lax.Precision.HIGHEST
    weights = spec_weight.astype(jnp.float32).reshape(spec_weight.shape[:4] + (C, C))
    real_d = grad_scaled[..., 0]
    imag_d = grad_scaled[..., 1]
    form = "xyzio,boxyz->bixyz"
    real_g = jnp.einsum(form, weights[0], real_d, precision=highest) + jnp.einsum(
        form, weights[1], imag_d, precision=highest
    )
    imag_g = jnp.einsum(form, weights[0], imag_d, precision=highest) - jnp.einsum(
        form, weights[1], real_d, precision=highest
    )
    return jnp.stack([real_g, imag_g], axis=-1).astype(jnp.bfloat16)


def on_device(fields, pre_act, cotangent, spec_weight, point_weight):
    count_x = lax.axis_size("gx")
    count_y = lax.axis_size("gy")
    local_batch, channels, local_x, local_yz = fields.shape
    local_y = local_yz // NZ
    sub_y = local_y // count_x
    local_mx = spec_weight.shape[1]
    local_mz = spec_weight.shape[3]
    stack_rows = 2 * local_batch * channels
    half_rows = local_batch * channels
    grad_pre = (cotangent.astype(jnp.float32) * gelu_slope(pre_act.astype(jnp.float32))).astype(
        jnp.bfloat16
    )
    stacked = jnp.concatenate([fields, grad_pre], axis=0)
    z_forward = z_forward_table()
    z_local = jnp.dot(
        stacked.reshape(stack_rows, local_x, local_y, NZ),
        z_forward,
        preferred_element_type=jnp.float32,
    ).astype(jnp.bfloat16)
    arrived = lax.all_to_all(
        z_local.reshape(stack_rows, local_x, local_y * 2 * MZ),
        "gx",
        split_axis=2,
        concat_axis=1,
        tiled=True,
    )
    z_spectra = arrived.reshape(stack_rows, NX, sub_y, MZ, 2)
    x_spectra = jnp.einsum(
        "sxyzr,xrkq->skyzq", z_spectra, forward_table(MX, NX), preferred_element_type=jnp.float32
    ).astype(jnp.bfloat16)
    x_spectra = x_spectra.reshape(stack_rows, MX, sub_y, 2 * MZ)
    mode_lines = lax.all_to_all(
        lax.all_to_all(x_spectra, "gx", split_axis=1, concat_axis=2, tiled=True),
        "gy",
        split_axis=3,
        concat_axis=2,
        tiled=True,
    )
    mode_lines = mode_lines.reshape(stack_rows, local_mx, NY, local_mz, 2)
    spectrum = jnp.einsum(
        "skyzr,yrlq->sklzq", mode_lines, forward_table(MY, NY), preferred_element_type=jnp.float32
    ).astype(jnp.bfloat16)
    spectrum = spectrum.reshape(2, local_batch, channels, local_mx, MY, local_mz, 2)
    field_hat = spectrum[0]
    grad_hat_in = spectrum[1]
    kz_index = lax.axis_index("gy") * local_mz + jnp.arange(local_mz, dtype=jnp.int32)
    weight_z = jnp.where(kz_index == 0, 1.0, 2.0).astype(jnp.float32) / float(NX * NY * NZ)
    grad_scaled = scale_modes(grad_hat_in, weight_z)
    grad_spec = lax.psum(weight_grads(field_hat, grad_scaled).astype(jnp.bfloat16), "dp").astype(
        jnp.float32
    )
    grad_hat = input_grads(spec_weight, grad_scaled).reshape(half_rows, local_mx, MY, local_mz, 2)
    span = count_y * sub_y
    order = jnp.arange(NY, dtype=jnp.int32)
    block = order // span
    rest = order % span
    positions = rest // sub_y * local_y + block * sub_y + rest % sub_y
    back_y = jnp.einsum(
        "sklzr,lryq->skyzq",
        grad_hat,
        inverse_table(MY, NY, positions),
        preferred_element_type=jnp.float32,
    ).astype(jnp.bfloat16)
    back_y = back_y.reshape(half_rows, local_mx, NY, 2 * local_mz)
    spread = lax.all_to_all(
        lax.all_to_all(back_y, "gx", split_axis=2, concat_axis=1, tiled=True),
        "gy",
        split_axis=2,
        concat_axis=3,
        tiled=True,
    )
    spread = spread.reshape(half_rows, MX, sub_y, MZ, 2)
    back_x = jnp.einsum(
        "skyzr,krxq->sxyzq",
        spread,
        inverse_table(MX, NX, jnp.arange(NX, dtype=jnp.int32)),
        preferred_element_type=jnp.float32,
    ).astype(jnp.bfloat16)
    returned = lax.all_to_all(
        back_x.reshape(half_rows, NX, sub_y * 2 * MZ), "gx", split_axis=1, concat_axis=2, tiled=True
    )
    spectral = jnp.dot(
        returned.reshape(half_rows, local_x, local_y, 2 * MZ),
        z_inverse_table(),
        preferred_element_type=jnp.float32,
    )
    spectral = spectral.reshape(local_batch, channels, local_x, local_yz)
    pointwise = jnp.einsum(
        "io,boxq->bixq", point_weight, grad_pre, preferred_element_type=jnp.float32
    )
    grad_fields = (spectral + pointwise).astype(jnp.bfloat16)
    return (grad_fields, grad_spec)


def solution(mesh):
    placed = (
        P("dp", None, "gx", "gy"),
        P("dp", None, "gx", "gy"),
        P("dp", None, "gx", "gy"),
        P(None, "gx", None, "gy", None),
        P(),
    )
    return jax.shard_map(
        on_device,
        mesh=mesh,
        in_specs=placed,
        out_specs=(P("dp", None, "gx", "gy"), P(None, "gx", None, "gy", None)),
        check_vma=False,
    )
```

profile of v0, /device:TPU:0, one launch (start us, length us, event | category | flops | bytes accessed | tf_op | source)
XLA Modules:
  0.0 1759.2 jit_solution(1794069897698833033)
XLA Ops:
  7.3 19.2 %fusion.8 = bf16[1,16,32,16384]{3,2,1,0:T(8,128)(2,1)} fusion(bf16[1,16,32,16384]{3,2,1,0:T(8,128)(2,1)} %param.6, bf16[1,16,32,16384]{3,2,1,0:T(8,128)(2,1)} %param.7), kind=kLoop, calls=%fused_computation.15 | loop fusion | flops 100663296 | bytes 50331648 | tf_op jit(solution)/shard_map/convert_element_type | solution.py:116
  26.4 22.9 %pad_maximum_fusion = bf16[2,16,32,16384]{3,2,1,0:T(8,128)(2,1)} fusion(bf16[1,16,32,16384]{3,2,1,0:T(8,128)(2,1)} %fusion.8, bf16[1,16,32,16384]{3,2,1,0:T(8,128)(2,1)} %param.5), kind=kLoop, calls=%fused_computation.12 | loop fusion | flops 16777216 | bytes 67108864 | tf_op jit(solution)/shard_map/concatenate | solution.py:119
  49.3 79.6 %reshape.892 = bf16[32,32,256,64]{3,2,1,0:T(8,128)(2,1)} reshape(bf16[2,16,32,16384]{3,2,1,0:T(8,128)(2,1)} %pad_maximum_fusion) | data formatting | bytes 67108864 | tf_op jit(solution)/shard_map/reshape | solution.py:122
  129.0 33.7 %convolution_convert_fusion = bf16[32,32,256,32]{2,3,1,0:T(8,128)(2,1)} fusion(bf16[32,32,256,64]{3,2,1,0:T(8,128)(2,1)} %reshape.892, bf16[64,32,1,1]{0,1,3,2:T(8,128)(2,1)S(1)} %bitcast.239), kind=kOutput, calls=%fused_computation.22 | convolution fusion | flops 1082130432 | bytes 50335744 | tf_op jit(solution)/shard_map/dot_general | solution.py:121
  162.7 110.3 %copy.282 = bf16[32,32,256,32]{1,0,3,2:T(8,128)(2,1)} copy(bf16[32,32,256,32]{2,3,1,0:T(8,128)(2,1)} %convolution_convert_fusion) | data formatting | bytes 33554432 | tf_op jit(solution)/shard_map/reshape | solution.py:127
  273.0 100.6 %reshape.933 = bf16[8,2,524288]{2,1,0:T(2,128)(2,1)} reshape(bf16[8192,32,32]{2,1,0:T(8,128)(2,1)} %bitcast.202) | data formatting | bytes 33554432
  381.6 362.7 %all-to-all-done = bf16[8,2,524288]{2,1,0:T(2,128)(2,1)} async-done(((bf16[8,2,524288]{2,1,0:T(2,128)(2,1)}), bf16[8,2,524288]{2,1,0:T(2,128)(2,1)}, u32[]{:S(2)}, u32[]{:S(2)}) %all-to-all-start) | async-done | bytes 16777248 | tf_op jit(solution)/shard_map/all_to_all | solution.py:126
  744.3 73.8 %reshape.934 = bf16[8192,32,32]{2,1,0:T(8,128)(2,1)} reshape(bf16[8,2,524288]{2,1,0:T(2,128)(2,1)} %all-to-all-done) | data formatting | bytes 33554432
  818.0 106.0 %copy.304 = bf16[32,32,8,1024]{1,2,0,3:T(8,128)(2,1)} copy(bf16[32,32,8,1024]{1,0,3,2:T(8,128)(2,1)} %bitcast.32) | data formatting | bytes 33554432 | tf_op jit(solution)/shard_map/all_to_all | solution.py:126
  924.1 77.7 %reshape.894 = bf16[32,256,32,16,2]{1,0,4,3,2:T(8,128)(2,1)} reshape(bf16[32,8,32,1024]{2,1,0,3:T(8,128)(2,1)} %bitcast.217) | data formatting | bytes 33554432 | tf_op jit(solution)/shard_map/reshape | solution.py:133
  1001.8 34.4 %fusion.13 = bf16[32,32,32,16,2]{2,1,3,0,4:T(8,128)(2,1)} fusion(bf16[32,256,32,16,2]{1,0,4,3,2:T(8,128)(2,1)} %reshape.894, bf16[256,1,32,2]{0,2,1,3:T(8,128)(2,1)S(1)} %get-tuple-element.39, bf16[256,1,32,2]{0,2,1,3:T(8,128)(2,1)S(1)} %get-tuple-element.38), kind=kOutput, calls=%fused_computation.23 | convolution fusion | flops 1074921472 | bytes 18939904 | tf_op jit(solution)/shard_map/sxyzr,xrkq->skyzq/dot_general | solution.py:134
  1045.5 9.8 copy.306
  1055.3 11.2 reshape.935
  1075.9 42.8 %all-to-all-done.1 = bf16[8,2,65536]{2,1,0:T(2,128)(2,1)S(1)} async-done(((bf16[8,2,65536]{2,1,0:T(2,128)(2,1)}), bf16[8,2,65536]{2,1,0:T(2,128)(2,1)S(1)}, u32[]{:S(2)}, u32[]{:S(2)}) %all-to-all-start.1) | async-done | bytes 2097184 | tf_op jit(solution)/shard_map/all_to_all | solution.py:139
  1125.6 16.3 copy.305
  1141.9 9.9 all_to_all.76
  1178.3 12.0 copy.223
  1190.3 11.4 reshape.937
  1205.6 26.0 %all-to-all-done.3 = bf16[8,2,32768]{2,1,0:T(2,128)(2,1)S(1)} async-done(((bf16[8,2,32768]{2,1,0:T(2,128)(2,1)}), bf16[8,2,32768]{2,1,0:T(2,128)(2,1)S(1)}, u32[]{:S(2)}, u32[]{:S(2)}) %all-to-all-start.3) | async-done | bytes 1048608 | tf_op jit(solution)/shard_map/all_to_all | solution.py:172
  1239.1 12.4 copy.225
  1273.0 13.8 copy.285
  1286.8 12.2 copy.228
  1305.9 11.4 copy.229
  1317.2 13.6 copy.230
  1342.9 41.4 %all-reduce.2.cloned.1.call-done = bf16[2,4,32,8,256]{4,3,2,1,0:T(8,128)(2,1)} async-done(((bf16[2,4,32,8,256]{4,3,2,1,0:T(8,128)(2,1)}), bf16[2,4,32,8,256]{4,3,2,1,0:T(8,128)(2,1)}) %all-reduce.2.cloned.1.call-update) | async-done | bytes 1048592 | tf_op jit(solution)/shard_map/psum | solution.py:155
  1387.0 132.4 %all-to-all-done.5 = bf16[16,256,1024]{2,0,1:T(8,128)(2,1)} async-done(((bf16[16,256,1024]{2,0,1:T(8,128)(2,1)}), bf16[16,256,1024]{2,0,1:T(8,128)(2,1)}, u32[]{:S(2)}, u32[]{:S(2)}) %all-to-all-start.5) | async-done | bytes 8388640 | tf_op jit(solution)/shard_map/all_to_all | solution.py:185
  1519.4 11.3 copy.232
  1530.7 39.1 %reshape.902 = bf16[16,32,256,32]{3,2,1,0:T(8,128)(2,1)} reshape(bf16[16,32,8,1024]{3,2,1,0:T(8,128)(2,1)} %copy.232) | data formatting | bytes 16777216 | tf_op jit(solution)/shard_map/reshape | solution.py:189
  1569.8 33.2 %fusion.97 = f32[16,32,256,64]{3,2,1,0:T(8,128)} fusion(bf16[16,32,256,32]{3,2,1,0:T(8,128)(2,1)} %reshape.902, bf16[32,64,1,1]{1,0,3,2:T(8,128)(2,1)S(1)} %bitcast.240), kind=kOutput, calls=%fused_computation.187 | convolution fusion | flops 536870912 | bytes 41947136 | tf_op jit(solution)/shard_map/dot_general | solution.py:188
  1603.0 48.9 %reshape.903 = f32[1,16,32,16384]{3,2,1,0:T(8,128)} reshape(f32[16,32,256,64]{3,2,1,0:T(8,128)} %fusion.97) | data formatting | bytes 67108864 | tf_op jit(solution)/shard_map/reshape | solution.py:193
  1651.9 81.6 %fusion.7 = bf16[1,16,32,16384]{3,1,2,0:T(8,128)(2,1)} fusion(f32[1,16,32,16384]{3,2,1,0:T(8,128)} %reshape.903, bf16[16,32,16384]{2,1,0:T(8,128)(2,1)} %bitcast.220, bf16[16,16]{1,0:T(8,128)(2,1)S(1)} %copy-done), kind=kOutput, calls=%fused_computation.14 | convolution fusion | flops 285212672 | bytes 67109376 | tf_op jit(solution)/shard_map/io,boxq->bixq/dot_general | solution.py:194
  1733.5 18.5 %copy.240 = bf16[1,16,32,16384]{3,2,1,0:T(8,128)(2,1)} copy(bf16[1,16,32,16384]{3,1,2,0:T(8,128)(2,1)} %fusion.7) | data formatting | bytes 33554432
  (59 shorter events, 114.4 us)
Async XLA Ops:
  7.2 1644.7 %copy-start = (bf16[16,16]{1,0:T(8,128)(2,1)S(1)}, bf16[16,16]{1,0:T(8,128)(2,1)}, u32[]{:S(2)}) copy-start(bf16[16,16]{1,0:T(8,128)(2,1)} %param.9) | copy-start | bytes 1540
  373.6 370.7 %all-to-all-start = ((bf16[8,2,524288]{2,1,0:T(2,128)(2,1)}), bf16[8,2,524288]{2,1,0:T(2,128)(2,1)}, u32[]{:S(2)}, u32[]{:S(2)}) async-start(bf16[8,2,524288]{2,1,0:T(2,128)(2,1)} %reshape.933), calls=%async_computation | async-start | bytes 33554432 | tf_op jit(solution)/shard_map/all_to_all | solution.py:126
  1066.5 52.1 %all-to-all-start.1 = ((bf16[8,2,65536]{2,1,0:T(2,128)(2,1)}), bf16[8,2,65536]{2,1,0:T(2,128)(2,1)S(1)}, u32[]{:S(2)}, u32[]{:S(2)}) async-start(bf16[8,2,65536]{2,1,0:T(2,128)(2,1)} %reshape.935), calls=%async_computation.1 | async-start | bytes 4194304 | tf_op jit(solution)/shard_map/all_to_all | solution.py:139
  1153.4 17.8 %copy-start.1 = (bf16[1,4,32,8,256]{2,4,3,1,0:T(8,128)(2,1)S(1)}, bf16[1,4,32,8,256]{2,4,3,1,0:T(8,128)(2,1)}, u32[]{:S(2)}) copy-start(bf16[1,4,32,8,256]{2,4,3,1,0:T(8,128)(2,1)} %copy.288) | copy-start | bytes 1572868
  1201.7 29.8 %all-to-all-start.3 = ((bf16[8,2,32768]{2,1,0:T(2,128)(2,1)}), bf16[8,2,32768]{2,1,0:T(2,128)(2,1)S(1)}, u32[]{:S(2)}, u32[]{:S(2)}) async-start(bf16[8,2,32768]{2,1,0:T(2,128)(2,1)} %reshape.937), calls=%async_computation.3 | async-start | bytes 2097152 | tf_op jit(solution)/shard_map/all_to_all | solution.py:172
  1330.8 188.6 %all-to-all-start.5 = ((bf16[16,256,1024]{2,0,1:T(8,128)(2,1)}), bf16[16,256,1024]{2,0,1:T(8,128)(2,1)}, u32[]{:S(2)}, u32[]{:S(2)}) async-start(bf16[16,256,1024]{2,0,1:T(8,128)(2,1)} %copy.230), calls=%async_computation.5 | async-start | bytes 16777216 | tf_op jit(solution)/shard_map/all_to_all | solution.py:185
  1335.8 48.5 %all-reduce.2.cloned.1.call-start = ((), (), s32[]{:S(2)}) async-start(), calls=%async_computation.6 | async-start | bytes 2097152 | tf_op jit(solution)/shard_map/psum | solution.py:155
Sparse Core Ops, SparseCore 0:
  1342.9 41.3 all-reduce.1
where the time goes:
time: 1770 us; the launch traced here: 1760 us
  local copies, waits for them, and re-layouts  860 us (49%)
  waiting for transfers between devices  605 us (34%)
  matrix products  193 us (11%)
  other arithmetic  56.5 us (3%)
  starting transfers between devices  20 us (1%)
    all_to_all x1, waiting for transfers between devices, on_device(): lax.all_to_all(z_local.reshape(stack_rows, local_x, local_y * 2 * MZ), 'g...  363 us
    unnamed x16, local copies, waits for them, and re-layouts  243 us
    all_to_all x1, waiting for transfers between devices, on_device(): lax.all_to_all(back_x.reshape(half_rows, NX, sub_y * 2 * MZ), 'gx', split...  132 us
    reshape x1, local copies, waits for them, and re-layouts, on_device(): z_local.reshape(stack_rows, local_x, local_y * 2 * MZ)  110 us
    all_to_all x1, local copies, waits for them, and re-layouts, on_device(): lax.all_to_all(z_local.reshape(stack_rows, local_x, local_y * 2 * MZ), 'g...  106 us
    dot_general x1, matrix products, on_device(): jnp.einsum('io,boxq->bixq', point_weight, grad_pre, preferred_element_typ...  81.6 us
    reshape x1, local copies, waits for them, and re-layouts, on_device(): stacked.reshape(stack_rows, local_x, local_y, NZ)  79.6 us
    reshape x1, local copies, waits for them, and re-layouts, on_device(): z_spectra = arrived.reshape(stack_rows, NX, sub_y, MZ, 2)  77.7 us
  transfers between devices with their start and end apart: 5, of which 5 were waited for; matrix products, arithmetic and copies ran while one was open for 1% of the time, Pallas kernels for 0%

commit v1 on v0

v1 whole, which is shorter than its diff:
```python
import functools
import math

import jax
import jax.numpy as jnp
import ml_dtypes
import numpy as np
from jax import lax
from jax.experimental import pallas as pl
from jax.experimental.pallas import tpu as pltpu
from jax.sharding import PartitionSpec as P

NZ = 64
ZGROUP = 4
VMEM_LIMIT = 56 * 1024 * 1024
BF16 = jnp.bfloat16
F32 = jnp.float32


def angles(kept, length, both_signs):
    freqs = np.arange(kept)
    if both_signs:
        freqs = np.where(freqs < kept // 2, freqs, length - kept + freqs)
    turns = np.arange(length)[:, None] * freqs[None, :] % length
    return (turns.astype(np.float32) * np.float32(2.0 * math.pi / length)).astype(np.float64)


def rounded(table):
    return np.asarray(table, np.float32).astype(ml_dtypes.bfloat16)


def forward_table(kept, length):
    angle = angles(kept, length, True)
    cosine, sine = np.cos(angle), np.sin(angle)
    upper = np.stack([cosine, -sine], axis=-1)
    lower = np.stack([sine, cosine], axis=-1)
    return np.stack([upper, lower], axis=1)


def z_table(kept, length, group):
    angle = angles(kept, length, False)
    parts = np.stack([np.cos(angle), -np.sin(angle)], axis=-1)
    table = np.einsum("zkr,yw->kyrwz", parts, np.eye(group))
    return rounded(table.reshape(kept * group * 2, group * length))


def x_tables(kept, length, count, channels):
    table = forward_table(kept, length).reshape(count, length // count, 2, kept, 2)
    big = np.einsum("dxrkq,ce->drcxkqe", table, np.eye(channels))
    rows = 2 * channels * (length // count)
    return rounded(big.reshape(count, rows, kept * 2 * channels))


def y_tables(kept, length, count):
    table = forward_table(kept, length).reshape(count, length // count, 2, kept, 2)
    return rounded(table.transpose(0, 4, 3, 1, 2).reshape(count, 2 * kept, -1))


def gelu_slope(value):
    size = jnp.abs(value)
    t = 1.0 / (1.0 + (0.3275911 / math.sqrt(2.0)) * size)
    decay = jnp.exp(value * value * -0.5)
    half_poly = t * (
        0.5 * 0.254829592
        + t
        * (
            0.5 * -0.284496736
            + t * (0.5 * 1.421413741 + t * (0.5 * -1.453152027 + t * (0.5 * 1.061405429)))
        )
    )
    lower = decay * (half_poly - size * (1.0 / math.sqrt(2.0 * math.pi)))
    return jnp.where(value < 0.0, lower, 1.0 - lower)


def dot(a, b, ca=1, cb=0):
    return lax.dot_general(a, b, (((ca,), (cb,)), ((), ())), preferred_element_type=F32)


def forward_kernel(dims, f_ref, p_ref, c_ref, zt_ref, yt_ref, xt_ref, gp_ref, out_ref, zs, ys):
    rows, block, kz_count, ky_count, row_block = dims
    chunk = pl.program_id(0)
    width = 2 * ZGROUP * NZ
    half = ZGROUP * NZ
    row_parts = rows // row_block
    piece = 16

    def body(step, carry):
        sub = step // row_parts
        part = step % row_parts
        lane = pl.multiple_of(sub * width, width)
        top = pl.multiple_of(part * row_block, row_block)
        for i in range(row_block // piece):
            at = (pl.ds(pl.multiple_of(top + i * piece, piece), piece), pl.ds(lane, width))
            slope = gelu_slope(p_ref[at].astype(F32))
            gp_ref[at] = (c_ref[at].astype(F32) * slope).astype(BF16)
        at = (pl.ds(top, row_block), pl.ds(lane, width))
        data = jnp.concatenate([f_ref[at], gp_ref[at]], axis=0)
        zt = zt_ref[...]
        spectra = [
            dot(zt, data[:, h * half : (h + 1) * half], 1, 1).reshape(
                kz_count, 2 * ZGROUP, 2 * row_block
            )
            for h in range(2)
        ]
        both = jnp.concatenate(spectra, axis=1).astype(BF16)
        line = chunk * (block // NZ * 2) + sub * (4 * ZGROUP)
        line = pl.multiple_of(line, 4 * ZGROUP)
        for kind in range(2):
            column = pl.multiple_of(kind * rows + top, row_block)
            zs[:, pl.ds(line, 4 * ZGROUP), pl.ds(column, row_block)] = both[
                :, :, kind * row_block : (kind + 1) * row_block
            ]
        return carry

    lax.fori_loop(0, (block // width) * row_parts, body, 0)

    @pl.when(chunk == pl.num_programs(0) - 1)
    def _():
        yt = yt_ref[...]

        def along_y(kz, carry):
            lines = dot(yt, zs[kz]).astype(BF16)
            top = pl.multiple_of(kz * ky_count, ky_count)
            for kind in range(2):
                for part in range(2):
                    ys[kind, pl.ds(top, ky_count), part * rows : (part + 1) * rows] = lines[
                        part * ky_count : (part + 1) * ky_count, kind * rows : (kind + 1) * rows
                    ]
            return carry

        lax.fori_loop(0, kz_count, along_y, 0)
        count_x, count_y, _, lines, lanes = out_ref.shape
        step = max(lanes, 256) // lanes
        for kind in range(2):
            for first in range(0, count_x, step):
                modes = dot(ys[kind], xt_ref[:, first * lanes : (first + step) * lanes])
                modes = modes.astype(BF16)
                for j in range(step):
                    out_ref[first + j, :, kind] = modes[:, j * lanes : (j + 1) * lanes].reshape(
                        count_y, lines, lanes
                    )


def modes_kernel(s_ref, own_ref, w_ref, e_ref, f_ref, spec_ref, hat_ref):
    n = f_ref.shape[0]

    def spread(values):
        wide = dot(values, e_ref[...])
        return [wide[:, j * n : (j + 1) * n] for j in range(4)]

    real = imag = 0.0
    for sample in range(s_ref.shape[0]):
        ur, ui, dr, di = spread(s_ref[sample])
        real = real + (ur * dr + ui * di)
        imag = imag + (ur * di - ui * dr)
    spec_ref[0] = real
    spec_ref[1] = imag
    _, _, dr, di = spread(own_ref[...])
    wr, wi = w_ref[0].astype(F32), w_ref[1].astype(F32)

    def over_outputs(terms):
        high = terms.astype(BF16)
        low = (terms - high.astype(F32)).astype(BF16)
        return dot(high, f_ref[...]) + dot(low, f_ref[...])

    hat_ref[...] = jnp.concatenate(
        [over_outputs(wr * dr + wi * di), over_outputs(wr * di - wi * dr)], axis=1
    ).astype(BF16)


def inverse_kernel(dims, g_ref, xt_ref, yi_ref, zi_ref, pw_ref, gp_ref, out_ref, gs, bs, zs):
    rows, block, kz_count, ky_count = dims
    chunk = pl.program_id(0)
    width = 2 * ZGROUP * NZ

    @pl.when(chunk == 0)
    def _():
        count_x, count_y, lines, lanes = g_ref.shape
        for d in range(count_x):
            gs[:, d * lanes : (d + 1) * lanes] = g_ref[d].reshape(count_y * lines, lanes)
        wide = min(256, rows)
        for part in range(2):
            for first in range(0, rows, wide):
                top = part * rows + first
                cells = dot(gs[...], xt_ref[top : top + wide, :], 1, 1).astype(BF16)
                bs[:, part * ky_count : (part + 1) * ky_count, first : first + wide] = (
                    cells.reshape(kz_count, ky_count, wide)
                )

        def along_y(kz, carry):
            zs[kz] = dot(yi_ref[...], bs[kz]).astype(BF16)
            return carry

        lax.fori_loop(0, kz_count, along_y, 0)

    def body(sub, carry):
        lane = pl.multiple_of(sub * width, width)
        line = chunk * (block // NZ * 2) + sub * (4 * ZGROUP)
        line = pl.multiple_of(line, 4 * ZGROUP)
        modes = zs[:, pl.ds(line, 4 * ZGROUP), :].reshape(kz_count * 4 * ZGROUP, rows)
        spectral = dot(modes, zi_ref[...], 0, 0)
        pointwise = dot(pw_ref[...], gp_ref[:, pl.ds(lane, width)])
        out_ref[:, pl.ds(lane, width)] = (spectral + pointwise).astype(BF16)
        return carry

    lax.fori_loop(0, block // width, body, 0)


def whole_block(shape):
    return pl.BlockSpec(shape, lambda *_: (0,) * len(shape))


def params():
    return pltpu.CompilerParams(
        dimension_semantics=("arbitrary",), vmem_limit_bytes=VMEM_LIMIT
    )


def on_device(fields, pre_act, cotangent, spec_weight, point_weight):
    count_x = lax.axis_size("gx")
    count_y = lax.axis_size("gy")
    _, channels, local_x, local_yz = fields.shape
    _, local_mx, my, local_mz, pairs = spec_weight.shape
    mx, mz = local_mx * count_x, local_mz * count_y
    nx = local_x * count_x
    local_y = local_yz // NZ
    ny = local_y * count_y
    rows = channels * local_x
    row_block = min(128, rows)
    block = min(1024, local_yz)
    lanes = local_mx * 2 * channels
    lines = local_mz * my
    modes = local_mx * my * local_mz
    at_x, at_y = lax.axis_index("gx"), lax.axis_index("gy")
    x_table = lax.dynamic_index_in_dim(
        jnp.asarray(x_tables(mx, nx, count_x, channels)), at_x, 0, keepdims=False
    )
    y_all = y_tables(my, ny, count_y)
    y_table = lax.dynamic_index_in_dim(jnp.asarray(y_all), at_y, 0, keepdims=False)
    y_inverse = lax.dynamic_index_in_dim(
        jnp.asarray(np.ascontiguousarray(y_all.transpose(0, 2, 1))), at_y, 0, keepdims=False
    )
    z_forward = jnp.asarray(z_table(mz, NZ, ZGROUP))
    z_inverse = jnp.asarray(z_table(mz, NZ, 2 * ZGROUP))

    flat = [array.reshape(rows, local_yz) for array in (fields, pre_act, cotangent)]
    tile = pl.BlockSpec((rows, block), lambda i: (0, i))
    grad_pre, partial = pl.pallas_call(
        functools.partial(forward_kernel, (rows, block, mz, my, row_block)),
        grid=(local_yz // block,),
        in_specs=[tile, tile, tile]
        + [whole_block(t.shape) for t in (z_forward, y_table, x_table)],
        out_specs=[tile, whole_block((count_x, count_y, 2, lines, lanes))],
        out_shape=[
            jax.ShapeDtypeStruct((rows, local_yz), BF16),
            jax.ShapeDtypeStruct((count_x, count_y, 2, lines, lanes), BF16),
        ],
        scratch_shapes=[
            pltpu.VMEM((mz, 2 * local_y, 2 * rows), BF16),
            pltpu.VMEM((2, mz * my, 2 * rows), BF16),
        ],
        compiler_params=params(),
        name="forward",
    )(*flat, z_forward, y_table, x_table)

    got = lax.all_to_all(partial, "gy", split_axis=1, concat_axis=1, tiled=True)
    summed = jnp.sum(got.astype(F32), axis=1).astype(BF16)
    got = lax.all_to_all(summed, "gx", split_axis=0, concat_axis=0, tiled=True)
    spectrum = jnp.sum(got.astype(F32), axis=0).astype(BF16)
    spectrum = spectrum.reshape(2, local_mz, my, local_mx, 2, channels)
    kz_index = at_y * local_mz + jnp.arange(local_mz, dtype=jnp.int32)
    weight_z = jnp.where(kz_index == 0, 1.0, 2.0).astype(F32) / float(nx * ny * NZ)
    weight = jnp.stack([jnp.ones_like(weight_z), weight_z], axis=0)
    spectrum = (spectrum.astype(F32) * weight[:, :, None, None, None, None]).astype(BF16)
    own = spectrum.transpose(3, 2, 1, 0, 4, 5).reshape(modes, 4 * channels)
    both = lax.all_gather(own, "dp", axis=0, tiled=False)

    eye = np.eye(channels)
    ones = np.ones((1, channels))
    by_input = np.kron(eye, ones)
    by_output = np.kron(ones, eye)
    expand = np.zeros((4 * channels, 4 * pairs))
    for j, part in enumerate((by_input, by_input, by_output, by_output)):
        expand[j * channels : (j + 1) * channels, j * pairs : (j + 1) * pairs] = part
    expand = jnp.asarray(rounded(expand))
    collect = jnp.asarray(rounded(by_input.T))
    weights = spec_weight.reshape(2, modes, pairs)
    part = min(256, modes)
    samples = both.shape[0]
    grad_spec, hat = pl.pallas_call(
        modes_kernel,
        grid=(modes // part,),
        in_specs=[
            pl.BlockSpec((samples, part, 4 * channels), lambda i: (0, i, 0)),
            pl.BlockSpec((part, 4 * channels), lambda i: (i, 0)),
            pl.BlockSpec((2, part, pairs), lambda i: (0, i, 0)),
            whole_block(expand.shape),
            whole_block(collect.shape),
        ],
        out_specs=[
            pl.BlockSpec((2, part, pairs), lambda i: (0, i, 0)),
            pl.BlockSpec((part, 2 * channels), lambda i: (i, 0)),
        ],
        out_shape=[
            jax.ShapeDtypeStruct((2, modes, pairs), F32),
            jax.ShapeDtypeStruct((modes, 2 * channels), BF16),
        ],
        compiler_params=params(),
        name="modes",
    )(both, own, weights, expand, collect)
    hat = hat.reshape(local_mx, my, local_mz, 2 * channels).transpose(2, 1, 0, 3)
    gathered = lax.all_gather(hat.reshape(lines, lanes), ("gx", "gy"), axis=0, tiled=False)
    gathered = gathered.reshape(count_x, count_y, lines, lanes)

    mixing = jnp.kron(point_weight, jnp.eye(local_x, dtype=BF16))
    grad_fields = pl.pallas_call(
        functools.partial(inverse_kernel, (rows, block, mz, my)),
        grid=(local_yz // block,),
        in_specs=[
            whole_block(t.shape) for t in (gathered, x_table, y_inverse, z_inverse, mixing)
        ]
        + [tile],
        out_specs=tile,
        out_shape=jax.ShapeDtypeStruct((rows, local_yz), BF16),
        scratch_shapes=[
            pltpu.VMEM((mz * my, count_x * lanes), BF16),
            pltpu.VMEM((mz, 2 * my, rows), BF16),
            pltpu.VMEM((mz, 2 * local_y, rows), BF16),
        ],
        compiler_params=params(),
        name="inverse",
    )(gathered, x_table, y_inverse, z_inverse, mixing, grad_pre)
    return (grad_fields.reshape(fields.shape), grad_spec.reshape(spec_weight.shape))


def solution(mesh):
    placed = (
        P("dp", None, "gx", "gy"),
        P("dp", None, "gx", "gy"),
        P("dp", None, "gx", "gy"),
        P(None, "gx", None, "gy", None),
        P(),
    )
    return jax.shard_map(
        on_device,
        mesh=mesh,
        in_specs=placed,
        out_specs=(P("dp", None, "gx", "gy"), P(None, "gx", None, "gy", None)),
        check_vma=False,
    )
```

time: 1770 us -> 218 us (0.12)
  local copies, waits for them, and re-layouts: 860 us -> 16.7 us
  waiting for transfers between devices: 605 us -> 60 us
  matrix products: 193 us -> 0 us
  Pallas kernels: 0 us -> 106 us
  other arithmetic: 56.5 us -> 2.21 us
    all_to_all x4 -> x1, waiting for transfers between devices: 564 us -> 26 us  [on_device(): got = lax.all_to_all(summed, 'gx', split_axis=0, concat_axis=0, tiled=True)]
    reshape x9 -> x1, local copies, waits for them, and re-layouts: 395 us -> 1.24 us  [on_device(): own = spectrum.transpose(3, 2, 1, 0, 4, 5).reshape(modes, 4 * channels)]
    unnamed x16 -> x4, local copies, waits for them, and re-layouts: 243 us -> 0.01 us
    all_to_all x11 -> x0, local copies, waits for them, and re-layouts: 197 us -> none  [the longest x1 106 us: on_device(): lax.all_to_all(z_local.reshape(stack_rows, local_x, local_y * 2 * MZ), 'g...]
    dot_general x7 -> x0, matrix products: 193 us -> none  [the longest x1 81.6 us: on_device(): jnp.einsum('io,boxq->bixq', point_weight, grad_pre, preferred_element_typ...]
    pallas_call x0 -> x3, Pallas kernels: none -> 106 us  [the longest x1 69 us: on_device(): pl.pallas_call(functools.partial(forward_kernel, (rows, block, mz, my, ro...]
    psum x1 -> x0, waiting for transfers between devices: 41.4 us -> none  [on_device(): lax.psum(weight_grads(field_hat, grad_scaled).astype(jnp.bfloat16), 'dp')]
    all_gather x0 -> x1, waiting for transfers between devices: none -> 34 us  [on_device(): lax.all_gather(hat.reshape(lines, lanes), ('gx', 'gy'), axis=0, tiled=False)]
  transfers between devices with their start and end apart: 5 -> 2, of which waited for: 5 -> 2; matrix products, arithmetic and copies ran while one was open for 1% -> 2% of each run, Pallas kernels for 0% -> 0%
where the time goes in v1:
time: 218 us; the launch traced here: 217 us
  Pallas kernels  106 us (49%)
  waiting for transfers between devices  60 us (28%)
  local copies, waits for them, and re-layouts  16.7 us (8%)
  between operations  14.1 us (6%)
  blocking collectives  11.1 us (5%)
  starting transfers between devices  7.28 us (3%)
  other arithmetic  2.21 us (1%)
    pallas_call x1, Pallas kernels, on_device(): pl.pallas_call(functools.partial(forward_kernel, (rows, block, mz, my, ro...  69 us
    all_gather x1, waiting for transfers between devices, on_device(): lax.all_gather(hat.reshape(lines, lanes), ('gx', 'gy'), axis=0, tiled=False)  34 us
    pallas_call x1, Pallas kernels, on_device(): pl.pallas_call(functools.partial(inverse_kernel, (rows, block, mz, my)),...  31.3 us
    all_to_all x1, waiting for transfers between devices, on_device(): got = lax.all_to_all(summed, 'gx', split_axis=0, concat_axis=0, tiled=True)  26 us
    all_to_all x1, starting transfers between devices, on_device(): got = lax.all_to_all(summed, 'gx', split_axis=0, concat_axis=0, tiled=True)  7.25 us
    all_gather x1, blocking collectives, on_device(): both = lax.all_gather(own, 'dp', axis=0, tiled=False)  5.64 us
    pallas_call x1, Pallas kernels, on_device(): pl.pallas_call(modes_kernel, grid=(modes // part,), in_specs=[pl.BlockSpe...  5.64 us
    all_to_all x1, blocking collectives, on_device(): got = lax.all_to_all(partial, 'gy', split_axis=1, concat_axis=1, tiled=True)  5.42 us
  transfers between devices with their start and end apart: 2, of which 2 were waited for; matrix products, arithmetic and copies ran while one was open for 2% of the time, Pallas kernels for 0%

profile of v1, /device:TPU:0, one launch (start us, length us, event | category | flops | bytes accessed | tf_op | source)
XLA Modules:
  0.0 217.3 jit_solution(2153586698068721220)
XLA Ops:
  7.2 1.5 dynamic-slice_bitcast_fusion.2.yt_ref
  8.6 3.1 %dynamic-slice_bitcast_fusion.xt_ref = bf16[1024,1024]{1,0:T(8,128)(2,1)} fusion(bf16[8,1024,1024]{2,1,0:T(8,128)(2,1)} %constant.51.clone, s32[]{:T(128)S(6)} %select_n.22), kind=kLoop, calls=%fused_computation | loop fusion | bytes 4194308 | tf_op jit(solution)/shard_map/jit(dynamic_index_in_dim)/squeeze | solution.py:235
  11.7 69.0 %forward.1 = (bf16[512,16384]{1,0:T(8,128)(2,1)}, bf16[8,2,2,256,128]{4,3,2,1,0:T(8,128)(2,1)}) custom-call(bf16[512,16384]{1,0:T(8,128)(2,1)} %bitcast.22, bf16[512,16384]{1,0:T(8,128)(2,1)} %bitcast.23, bf16[512,16384]{1,0:T(8,128)(2,1)} %bitcast.24, bf16[128,256]{1,0:T(8,128)(2,1)} %constant.54.clone.zt_ref, ...), custom_call_target="tpu_custom_call" | custom-call | tf_op jit(solution)/shard_map/forward/pallas_call | solution.py:248
  80.7 1.7 copy.24
  82.4 5.4 %all_to_all.10 = bf16[8,2,2,256,128]{4,3,2,0,1:T(8,128)(2,1)S(1)} all-to-all(bf16[8,2,2,256,128]{4,3,2,0,1:T(8,128)(2,1)S(1)} %copy.24), channel_id=1, replica_groups=mesh['dp'=2,'gx'=8,'gy'=2] {'gy'}, dimensions={1} | all-to-all | bytes 4194304 | tf_op jit(solution)/shard_map/all_to_all | solution.py:266
  87.9 1.7 reduce_sum.24
  89.5 7.2 %all-to-all-start.1 = ((bf16[8,2,256,128]{3,2,1,0:T(8,128)(2,1)}), bf16[8,2,256,128]{3,2,1,0:T(8,128)(2,1)S(1)}, u32[]{:S(2)}, u32[]{:S(2)}) async-start(bf16[8,2,256,128]{3,2,1,0:T(8,128)(2,1)} %reduce_sum.24), calls=%async_computation.1 | async-start | bytes 2097152 | tf_op jit(solution)/shard_map/all_to_all | solution.py:268
  96.8 0.0 all-gather.2.cloned.1.call-start
  96.8 26.0 %all-to-all-done.1 = bf16[8,2,256,128]{3,2,1,0:T(8,128)(2,1)S(1)} async-done(((bf16[8,2,256,128]{3,2,1,0:T(8,128)(2,1)}), bf16[8,2,256,128]{3,2,1,0:T(8,128)(2,1)S(1)}, u32[]{:S(2)}, u32[]{:S(2)}) %all-to-all-start.1) | async-done | bytes 1048608 | tf_op jit(solution)/shard_map/all_to_all | solution.py:268
  122.8 0.1 reduce_sum.25
  123.0 0.1 copy.25
  123.1 0.3 reshape.74
  123.4 0.2 fusion
  123.6 1.7 copy.26
  125.3 1.2 reshape.68.own_ref
  126.6 0.5 all_gather_reshape.6
  127.1 0.1 copy.27
  127.2 0.0 copy-start.1
  127.2 5.6 %all_gather.6 = bf16[2,1024,64]{1,2,0:T(8,128)(2,1)S(1)} all-gather(bf16[1,1024,64]{1,2,0:T(8,128)(2,1)S(1)} %copy.27), channel_id=1, replica_groups=mesh['dp'=2,'gx'=8,'gy'=2] {'dp'}, dimensions={0}, use_global_device_ids=true | all-gather | bytes 393216 | tf_op jit(solution)/shard_map/all_gather | solution.py:276
  132.9 1.0 copy.29.s_ref
  133.9 5.6 %modes.1 = (f32[2,1024,256]{2,1,0:T(8,128)}, bf16[1024,32]{1,0:T(8,128)(2,1)}) custom-call(bf16[2,1024,64]{2,1,0:T(8,128)(2,1)} %copy.29.s_ref, bf16[1024,64]{1,0:T(8,128)(2,1)} %reshape.68.own_ref, bf16[2,1024,256]{2,1,0:T(8,128)(2,1)} %bitcast.27, bf16[64,1024]{1,0:T(8,128)(2,1)} %constant.56.clone.e_ref, bf16[256,16]{1,0:T(8,128)(2,1)} %constant.57.clone.f_ref), custom_call_target="tpu_custom_call" | custom-call | tf_op jit(solution)/shard_map/modes/pallas_call | solution.py:290
  139.5 1.2 copy.30
  140.7 0.8 all_gather_reshape.7
  141.5 0.0 all-gather.2.cloned.1.call-update
  141.5 0.0 copy-done.1
  141.5 0.0 copy-start
  141.5 0.2 broadcast_multiply_fusion
  141.7 2.8 %mul.41.pw_ref = bf16[512,512]{1,0:T(8,128)(2,1)} reshape(bf16[16,32,16,32]{3,2,1,0:T(8,128)(2,1)S(1)} %broadcast_multiply_fusion) | data formatting | bytes 1048576 | tf_op jit(solution)/shard_map/jit(kron)/mul | solution.py:315
  144.5 0.0 copy-done
  144.5 0.7 dynamic-slice_bitcast_fusion.1.yi_ref
  145.2 34.0 %all-gather.2.cloned.1.call-done = bf16[16,256,128]{2,1,0:T(8,128)(2,1)} async-done(((bf16[1,256,128]{2,1,0:T(8,128)(2,1)}), bf16[16,256,128]{2,1,0:T(8,128)(2,1)}) %all-gather.2.cloned.1.call-update) | async-done | bytes 1048592 | tf_op jit(solution)/shard_map/all_gather | solution.py:312
  179.1 31.3 %inverse.1 = bf16[512,16384]{1,0:T(8,128)(2,1)} custom-call(bf16[8,2,256,128]{3,2,1,0:T(8,128)(2,1)} %bitcast.26, bf16[1024,1024]{1,0:T(8,128)(2,1)} %dynamic-slice_bitcast_fusion.xt_ref, bf16[512,64]{1,0:T(8,128)(2,1)} %dynamic-slice_bitcast_fusion.1.yi_ref, bf16[256,512]{1,0:T(8,128)(2,1)} %constant.55.clone.zi_ref, bf16[512,512]{1,0:T(8,128)(2,1)} %mul.41.pw_ref, ...), custom_call_target="tpu_custom_call" | custom-call | tf_op jit(solution)/shard_map/inverse/pallas_call | solution.py:316
  (3 shorter events, 0.0 us)
Async XLA Ops:
  89.5 33.3 %all-to-all-start.1 = ((bf16[8,2,256,128]{3,2,1,0:T(8,128)(2,1)}), bf16[8,2,256,128]{3,2,1,0:T(8,128)(2,1)S(1)}, u32[]{:S(2)}, u32[]{:S(2)}) async-start(bf16[8,2,256,128]{3,2,1,0:T(8,128)(2,1)} %reduce_sum.24), calls=%async_computation.1 | async-start | bytes 2097152 | tf_op jit(solution)/shard_map/all_to_all | solution.py:268
  96.8 82.4 %all-gather.2.cloned.1.call-start = ((), (), s32[]{:S(2)}) async-start(), calls=%async_computation.2 | async-start | bytes 1114112 | tf_op jit(solution)/shard_map/all_gather | solution.py:312
  127.2 14.3 %copy-start.1 = (bf16[16,16]{1,0:T(8,128)(2,1)S(1)}, bf16[16,16]{1,0:T(8,128)(2,1)}, u32[]{:S(2)}) copy-start(bf16[16,16]{1,0:T(8,128)(2,1)} %param.16) | copy-start | bytes 1540
  141.5 3.0 %copy-start = (bf16[2,512,64]{2,1,0:T(8,128)(2,1)S(1)}, bf16[2,512,64]{2,1,0:T(8,128)(2,1)}, u32[]{:S(2)}) copy-start(bf16[2,512,64]{2,1,0:T(8,128)(2,1)} %constant.53.clone) | copy-start | bytes 393220
Sparse Core Ops, SparseCore 0:
  141.6 37.4 all-gather.1
